TPU v7x, 32 devices: a whole 2x2x4 slice. The times are simulated.
32 devices in a mesh: groups: 2 (over y), ctx: 4 (over z), head: 2 (over x), section: 2 (over core).
Axes of the slice: x: 2, y: 2, z: 4, core: 2. Of those that a mesh axis runs over, the one named last changes fastest.
Arguments:
- queries_in: bfloat16 [2, 2048, 1024], P('section', ('groups', 'ctx'), 'head'), parts along dimension 1, may hold values from -6 to 6
- keys_in: bfloat16 [2, 2048, 1024], P('section', ('groups', 'ctx'), 'head'), parts along dimension 1, may hold values from -6 to 6
- values_in: bfloat16 [2048, 2048], P(('groups', 'ctx'), 'head'), parts along dimension 0, may hold values from -6 to 6
- gate_in: bfloat16 [2, 2048, 2048], P('section', ('groups', 'ctx'), 'head'), parts along dimension 1, may hold values from -6 to 6
- decay_in: float32 [2, 2048, 16], P('section', ('groups', 'ctx'), 'head'), parts along dimension 1, may hold values from -3 to 3072
- write_in: float32 [2, 2048, 16], P('section', ('groups', 'ctx'), 'head'), parts along dimension 1, may hold values from -16 to 2
- decay_log: float32 [2, 16], P('section', 'head'), may hold values from -16 to -2
- conv_query: bfloat16 [2, 4, 1024], P('section', None, 'head'), may hold values from -3 to 3
- conv_key: bfloat16 [2, 4, 1024], P('section', None, 'head'), may hold values from -3 to 3
- conv_value: bfloat16 [2, 4, 2048], P('section', None, 'head'), may hold values from -3 to 3
- norm_gain: float32 [2, 128], P('section'), may hold values from 0.25 to 1.75
- segment_ids: int32 [2048], P(('groups', 'ctx')), parts along dimension 0, may hold values from 0 to 3, never falling along the last dimension, each value on 1 to 512 neighbouring positions
Outputs:
- layer_out: bfloat16 [2, 2048, 2048], P('section', ('groups', 'ctx'), 'head'), parts along dimension 1
There are 2 independent parts, one for each index of `groups`. A program takes and returns all parts, laid end to end along the dimension named above; an argument that names none is the same for every part. Nothing has to cross between parts.
All inputs are finite; a program needn't handle non-finite values.
Results may differ from a plain program's by a relative error of at most 0.0033.
Values may be sent and summed in bfloat16 or wider, within the bound.
A program may use at most 128 MiB of HBM per device.

v0:
```python
import jax
import jax.numpy as jnp
from jax import lax
from jax.sharding import PartitionSpec as P

DK = 128
DV = 128
CONV = 4
BLOCK = 64


highest_precision = lax.Precision.HIGHEST


def from_behind(block, axis, distance):
    devices = range(lax.axis_size(axis))
    route = [(i - distance, i) for i in devices if i - distance in devices]
    return lax.ppermute(block, axis, route)


def carried_in(value, axis, join, neutral):
    count, mine = (lax.axis_size(axis), lax.axis_index(axis))
    pieces = jax.tree.map(lambda part: lax.all_gather(part, axis), value)
    total = jax.tree.map(
        lambda part, zero: jnp.full_like(part, 0) + jnp.asarray(zero, part.dtype), value, neutral
    )

    def turn(position, total):
        longer = join(total, jax.tree.map(lambda part: part[position], pieces))
        return jax.tree.map(lambda new, old: jnp.where(position < mine, new, old), longer, total)

    return lax.fori_loop(0, count - 1, turn, total)


def conv_rows(extended, weight, extended_seg, own_seg):
    length = own_seg.shape[0]
    taps = weight.shape[0]
    summed = jnp.zeros((length, extended.shape[1]), jnp.float32)
    for offset in range(taps):
        keeping = (extended_seg[offset : offset + length] == own_seg)[:, None]
        summed = (
            summed
            + jnp.where(keeping, extended[offset : offset + length], 0.0)
            * weight[offset].astype(jnp.float32)[None, :]
        )
    return jax.nn.silu(summed)


def unit_rows(values):
    return values * lax.rsqrt(jnp.sum(values * values, axis=-1, keepdims=True) + 1e-06)


def compose(earlier, later):
    operator = jnp.einsum("hab,hbc->hac", later[0], earlier[0], precision=highest_precision)
    increment = (
        jnp.einsum("hab,hbc->hac", later[0], earlier[1], precision=highest_precision) + later[1]
    )
    return (operator, increment)


def local(
    queries_in,
    keys_in,
    values_in,
    gate_in,
    decay_in,
    write_in,
    decay_log,
    conv_query,
    conv_key,
    conv_value,
    norm_gain,
    segment_ids,
):
    length = segment_ids.shape[0]
    rim_rows = CONV - 1
    block = BLOCK
    count_blocks = length // block
    section_index = lax.axis_index("section")
    heads_value = decay_in.shape[2]
    seg_words = segment_ids.astype(jnp.bfloat16)
    ident_block = jnp.eye(block, dtype=jnp.float32)
    ident_key = jnp.eye(DK, dtype=jnp.float32)
    row_index = lax.broadcasted_iota(jnp.int32, (block, block), 0)
    col_index = lax.broadcasted_iota(jnp.int32, (block, block), 1)
    seg_blocks = segment_ids.reshape(count_blocks, block)
    same_doc = seg_blocks[:, :, None] == seg_blocks[:, None, :]
    causal_mask = (row_index >= col_index)[None] & same_doc
    strict_mask = row_index > col_index

    def mixer_part(extended_seg, unit_pair, params, count_value, value_part):
        taps_full, rate_full, decay_full, write_full, gate_full, gain = params
        query_unit, key_unit = unit_pair
        seg_before = extended_seg[rim_rows - 1]
        previous_seg = jnp.concatenate([seg_before[None], segment_ids[:-1]])
        block_prev = previous_seg.reshape(count_blocks, block)[:, 0]
        links_start = (seg_blocks == block_prev[:, None]).astype(jnp.float32)
        value_rim = from_behind(value_part[length - rim_rows :], "ctx", 1)
        values = conv_rows(
            jnp.concatenate([value_rim, value_part]).astype(jnp.float32),
            taps_full,
            extended_seg,
            segment_ids,
        )
        values_head = (
            values.reshape(length, count_value, DV)
            .transpose(1, 0, 2)
            .reshape(count_value, count_blocks, block, DV)
        )
        queries_head = (
            jnp.repeat(query_unit, 2, axis=1)
            .transpose(1, 0, 2)
            .reshape(count_value, count_blocks, block, DK)
        )
        keys_head = (
            jnp.repeat(key_unit, 2, axis=1)
            .transpose(1, 0, 2)
            .reshape(count_value, count_blocks, block, DK)
        )
        log_decay = -jnp.exp(rate_full)[None, :] * jax.nn.softplus(decay_full)
        cumulative = jnp.cumsum(log_decay.T.reshape(count_value, count_blocks, block), axis=2)
        betas = jax.nn.sigmoid(write_full).T.reshape(count_value, count_blocks, block)
        difference = cumulative[..., :, None] - cumulative[..., None, :]
        decay_pair = jnp.where(
            causal_mask[None], jnp.exp(jnp.where(causal_mask[None], difference, 0.0)), 0.0
        )
        from_start = jnp.exp(cumulative) * links_start[None]
        key_gram = jnp.einsum("hnid,hnjd->hnij", keys_head, keys_head, precision=highest_precision)
        lower_part = jnp.where(
            strict_mask[None, None], betas[..., None] * key_gram * decay_pair, 0.0
        )
        system = ident_block[None, None] + lower_part
        right_side = jnp.concatenate(
            [(betas * from_start)[..., None] * keys_head, betas[..., None] * values_head], axis=-1
        )
        solved = jax.scipy.linalg.solve_triangular(
            system, right_side, lower=True, unit_diagonal=True
        )
        weight_rows = solved[..., :DK]
        value_rows = solved[..., DK:]
        key_end = decay_pair[:, :, block - 1, :, None] * keys_head
        operator = from_start[:, :, block - 1][..., None, None] * ident_key[
            None, None
        ] - jnp.einsum("hnjd,hnje->hnde", key_end, weight_rows, precision=highest_precision)
        state_end = jnp.einsum("hnjd,hnje->hnde", key_end, value_rows, precision=highest_precision)
        mixing = decay_pair * jnp.einsum(
            "hnid,hnjd->hnij", queries_head, keys_head, precision=highest_precision
        )
        local_out = jnp.einsum("hnij,hnje->hnie", mixing, value_rows, precision=highest_precision)
        carry_map = from_start[..., None] * queries_head - jnp.einsum(
            "hnij,hnjd->hnid", mixing, weight_rows, precision=highest_precision
        )
        identity_pair = (
            jnp.broadcast_to(ident_key, (count_value, DK, DK)),
            jnp.zeros((count_value, DK, DV), jnp.float32),
        )

        def advance(carry, item):
            return (compose(carry, item), carry)

        total_pair, prefix_pair = lax.scan(
            advance,
            identity_pair,
            (operator.transpose(1, 0, 2, 3), state_end.transpose(1, 0, 2, 3)),
        )
        prefix_operator, start_state = carried_in(total_pair, "ctx", compose, identity_pair)
        block_start = (
            jnp.einsum("nhab,hbc->nhac", prefix_pair[0], start_state, precision=highest_precision)
            + prefix_pair[1]
        )
        mixed = local_out + jnp.einsum(
            "hnid,nhde->hnie", carry_map, block_start, precision=highest_precision
        )
        mixed = mixed.reshape(count_value, length, DV).transpose(1, 0, 2)
        norm_scale = lax.rsqrt(jnp.mean(mixed * mixed, axis=-1, keepdims=True) + 1e-06)
        gate_act = jax.nn.silu(gate_full.astype(jnp.float32)).reshape(length, count_value, DV)
        output = mixed * norm_scale * gain[None, None, :] * gate_act
        return output.reshape(length, count_value * DV).astype(jnp.bfloat16)

    rim_query, rim_key, rim_seg = from_behind(
        (
            queries_in[:, length - rim_rows :],
            keys_in[:, length - rim_rows :],
            seg_words[length - rim_rows :],
        ),
        "ctx",
        1,
    )
    extended_seg = jnp.concatenate([rim_seg.astype(jnp.int32), segment_ids])
    heads_key = queries_in.shape[2] // DK
    units = []
    query_unit = unit_rows(
        conv_rows(
            jnp.concatenate([rim_query[0], queries_in[0]]).astype(jnp.float32),
            conv_query[0],
            extended_seg,
            segment_ids,
        ).reshape(length, heads_key, DK)
    )
    key_unit = unit_rows(
        conv_rows(
            jnp.concatenate([rim_key[0], keys_in[0]]).astype(jnp.float32),
            conv_key[0],
            extended_seg,
            segment_ids,
        ).reshape(length, heads_key, DK)
    )
    units.append((query_unit, key_unit))
    extended_seg, units = (extended_seg, units)
    own_params = (conv_value[0], decay_log[0], decay_in[0], write_in[0], gate_in[0], norm_gain[0])
    first_out = mixer_part(extended_seg, units[0], own_params, heads_value, values_in)
    handed = from_behind(first_out, "section", 1)
    layer_input = jnp.where(section_index == 0, values_in, handed)
    mixer_result = mixer_part(extended_seg, units[0], own_params, heads_value, layer_input)
    return mixer_result[None]


def solution(mesh):
    placed = (
        P("section", ("groups", "ctx"), "head"),
        P("section", ("groups", "ctx"), "head"),
        P(("groups", "ctx"), "head"),
        P("section", ("groups", "ctx"), "head"),
        P("section", ("groups", "ctx"), "head"),
        P("section", ("groups", "ctx"), "head"),
        P("section", "head"),
        P("section", None, "head"),
        P("section", None, "head"),
        P("section", None, "head"),
        P("section", None),
        P(("groups", "ctx")),
    )
    return jax.shard_map(
        local,
        mesh=mesh,
        in_specs=placed,
        out_specs=P("section", ("groups", "ctx"), "head"),
        check_vma=False,
    )
```

profile of v0, /device:TPU:29, one launch (start us, length us, event | category | flops | bytes accessed | tf_op | source)
XLA Modules:
  0.0 507.5 jit_solution(16772065119456402239)
XLA Ops:
  29.6 2.9 fusion.57
  32.6 158.1 %custom-call.9 = f32[8,4,1,64,64]{3,4,2,1,0:T(8,128)S(1)} custom-call(f32[8,4,1,64,64]{4,3,2,1,0:T(8,128)} %fusion.57), custom_call_target="InvertDiagBlocksLowerTriangular" | custom-call | tf_op jit(solution)/shard_map/jit(_solve_triangular)/vmap(vmap())/triangular_solve | solution.py:136
  194.3 5.2 %convolution_bitcast_fusion.1 = f32[4,8,128,128]{3,2,0,1:T(8,128)} fusion(f32[8,4,64,256]{3,2,1,0:T(8,128)S(1)} %fusion.39, f32[8,4,64,128]{3,2,1,0:T(8,128)S(1)} %bitcast.226, f32[8,4,64]{2,1,0:T(4,128)S(1)} %bitcast.242), kind=kOutput, calls=%fused_computation.63 | convolution fusion | flops 402915328 | bytes 4210688 | tf_op jit(solution)/shard_map/hnjd,hnje->hnde/dot_general | solution.py:145
  199.5 5.3 %multiply_subtract_fusion.1 = f32[4,8,128,128]{3,2,0,1:T(8,128)} fusion(f32[128,128]{1,0:T(8,128)S(1)} %fusion.112, f32[4,8]{0,1:T(8,128)S(1)} %copy.101, f32[8,4,64,256]{3,2,1,0:T(8,128)S(1)} %fusion.39, f32[8,4,64,128]{3,2,1,0:T(8,128)S(1)} %bitcast.227, f32[8,4,64]{2,1,0:T(4,128)S(1)} %bitcast.243), kind=kOutput, calls=%fused_computation.49 | convolution fusion | flops 403963904 | bytes 4280320 | tf_op jit(solution)/shard_map/hnjd,hnje->hnde/dot_general | solution.py:144
  208.1 22.9 %while.62 = (s32[]{:T(128)}, f32[8,128,128]{2,1,0:T(8,128)S(1)}, f32[8,128,128]{2,1,0:T(8,128)S(1)}, f32[4,8,128,128]{3,2,1,0:T(8,128)}, f32[4,8,128,128]{2,3,1,...) while((s32[]{:T(128)}, f32[8,128,128]{2,1,0:T(8,128)S(1)}, ...), condition=%wide.region_4.6_spmd.clone, body=%wide.region_3.5_spmd.clone.sunk | while | flops 403046400 | bytes 9964136 | solution.py:161
  237.9 2.2 fusion.88
  240.1 2.3 convolution_subtract_fusion.1
  242.4 38.6 %all-gather.9.cloned.1.call-done = f32[32,128,128]{2,1,0:T(8,128)} async-done(((f32[8,128,128]{2,1,0:T(8,128)}), f32[32,128,128]{2,1,0:T(8,128)}) %all-gather.9.cloned.1.call-update) | async-done | bytes 2097168 | tf_op jit(solution)/shard_map/all_gather | solution.py:23
  281.1 46.2 %all-gather.11.cloned.1.call-done = f32[32,128,128]{2,1,0:T(8,128)} async-done(((f32[8,128,128]{2,1,0:T(8,128)}), f32[32,128,128]{2,1,0:T(8,128)}) %all-gather.11.cloned.1.call-update) | async-done | bytes 2097168 | tf_op jit(solution)/shard_map/all_gather | solution.py:23
  327.3 5.8 %while.63 = (s32[]{:T(128)}, f32[8,128,128]{2,1,0:T(8,128)S(1)}, s32[]{:T(128)}, f32[4,8,128,128]{3,2,1,0:T(8,128)}, f32[4,8,128,128]{3,2,1,0:T(8,128)}, /*index=5*/s32[]{:T(128)}, s32[]{:T(128)}) while((s32[]{:T(128)}, f32[8,128,128]{2,1,0:T(8,128)S(1)}, s32[]{:T(128)}, f32[4,8,128,128]{3,2,1,0:T(8,128)}, ...), condition=%wide.region_6.8_spmd.clone, body=%wide.region_5.7_spmd.clone.sunk | while | flops 201850880 | bytes 3672671 | solution.py:32
  333.2 4.4 bitcast_add_fusion.1
  337.6 4.2 fusion.46
  344.0 2.6 collective-permute-done.4
  349.2 2.9 collective-permute-done.5
  356.7 5.2 %convolution_bitcast_fusion = f32[4,8,128,128]{3,2,0,1:T(8,128)} fusion(f32[8,4,64,256]{3,2,1,0:T(8,128)S(1)} %fusion.38, f32[8,4,64,128]{3,2,1,0:T(8,128)S(1)} %bitcast.229, f32[8,4,64]{2,1,0:T(4,128)S(1)} %bitcast.244), kind=kOutput, calls=%fused_computation.62 | convolution fusion | flops 402915328 | bytes 4210688 | tf_op jit(solution)/shard_map/hnjd,hnje->hnde/dot_general | solution.py:145
  361.8 5.3 %multiply_subtract_fusion = f32[4,8,128,128]{3,2,0,1:T(8,128)} fusion(f32[128,128]{1,0:T(8,128)S(1)} %fusion.112, f32[4,8]{0,1:T(8,128)S(1)} %copy.101, f32[8,4,64,256]{3,2,1,0:T(8,128)S(1)} %fusion.38, f32[8,4,64,128]{3,2,1,0:T(8,128)S(1)} %bitcast.230, f32[8,4,64]{2,1,0:T(4,128)S(1)} %bitcast.245), kind=kOutput, calls=%fused_computation.48 | convolution fusion | flops 403963904 | bytes 4280320 | tf_op jit(solution)/shard_map/hnjd,hnje->hnde/dot_general | solution.py:144
  370.4 22.6 %while.64 = (s32[]{:T(128)}, f32[8,128,128]{2,1,0:T(8,128)S(1)}, f32[8,128,128]{2,1,0:T(8,128)S(1)}, f32[4,8,128,128]{3,2,1,0:T(8,128)}, f32[4,8,128,128]{2,3,1,...) while((s32[]{:T(128)}, f32[8,128,128]{2,1,0:T(8,128)S(1)}, ...), condition=%wide.region_9.11_spmd.clone, body=%wide.region_8.10_spmd.clone.sunk | while | flops 403046400 | bytes 9964136 | solution.py:161
  394.5 3.5 fusion.83
  398.0 3.5 convolution_subtract_fusion
  401.5 37.0 %all-gather.13.cloned.1.call-done = f32[32,128,128]{2,1,0:T(8,128)} async-done(((f32[8,128,128]{2,1,0:T(8,128)}), f32[32,128,128]{2,1,0:T(8,128)}) %all-gather.13.cloned.1.call-update) | async-done | bytes 2097168 | tf_op jit(solution)/shard_map/all_gather | solution.py:23
  438.5 46.1 %all-gather.15.cloned.1.call-done = f32[32,128,128]{2,1,0:T(8,128)} async-done(((f32[8,128,128]{2,1,0:T(8,128)}), f32[32,128,128]{2,1,0:T(8,128)}) %all-gather.15.cloned.1.call-update) | async-done | bytes 2097168 | tf_op jit(solution)/shard_map/all_gather | solution.py:23
  484.6 6.0 %while.65 = (s32[]{:T(128)}, f32[8,128,128]{2,1,0:T(8,128)S(1)}, s32[]{:T(128)}, f32[4,8,128,128]{3,2,1,0:T(8,128)}, f32[4,8,128,128]{3,2,1,0:T(8,128)}, /*index=5*/s32[]{:T(128)}, s32[]{:T(128)}) while((s32[]{:T(128)}, f32[8,128,128]{2,1,0:T(8,128)S(1)}, s32[]{:T(128)}, f32[4,8,128,128]{3,2,1,0:T(8,128)}, ...), condition=%wide.region_11.13_spmd.clone, body=%wide.region_10.12_spmd.clone.sunk | while | flops 201850880 | bytes 3672671 | solution.py:32
  490.6 3.7 bitcast_add_fusion
  494.4 4.2 fusion.49
  (229 shorter events, 108.6 us)
Async XLA Ops:
  6.5 20.4 %copy-start.23 = (bf16[1,256,512]{2,1,0:T(8,128)(2,1)S(1)}, bf16[1,256,512]{2,1,0:T(8,128)(2,1)}, u32[]{:S(2)}) copy-start(bf16[1,256,512]{2,1,0:T(8,128)(2,1)} %param.23) | copy-start | bytes 786436
  6.5 274.6 %all-gather.9.cloned.1.call-start = ((), (), s32[]{:S(2)}) async-start(), calls=%async_computation | async-start | bytes 2621440 | tf_op jit(solution)/shard_map/all_gather | solution.py:23
  7.3 14.5 %collective-permute-start = (bf16[3]{0:T(256)(128)(2,1)S(1)}, bf16[3]{0:T(256)(128)(2,1)S(1)}, u32[]{:S(2)}, u32[]{:S(2)}) collective-permute-start(bf16[3]{0:T(256)(128)(2,1)S(1)} %slice.169), channel_id=1, source_target_pairs={{0,4},{4,8},{8,12},{1,5},{5,9},{9,13},{2,6},{6,10},{10,14},{3,7},{... | collective-permute-start | bytes 26 | tf_op jit(solution)/shard_map/ppermute | solution.py:18
  9.3 16.5 %collective-permute-start.1 = (bf16[1,3,512]{2,1,0:T(4,128)(2,1)S(1)}, bf16[1,3,512]{2,1,0:T(4,128)(2,1)S(1)}, u32[]{:S(2)}, u32[]{:S(2)}) collective-permute-start(bf16[1,3,512]{2,1,0:T(4,128)(2,1)S(1)} %slice.171), channel_id=1, source_target_pairs={{0,4},{4,8},{8,12},{1,5},{5,9},{9,13},{2,6},{6,10},{10,14},{3,7},{... | collective-permute-start | bytes 9224 | tf_op jit(solution)/shard_map/ppermute | solution.py:18
  11.3 15.6 %collective-permute-start.2 = (bf16[1,3,512]{2,1,0:T(4,128)(2,1)S(1)}, bf16[1,3,512]{2,1,0:T(4,128)(2,1)S(1)}, u32[]{:S(2)}, u32[]{:S(2)}) collective-permute-start(bf16[1,3,512]{2,1,0:T(4,128)(2,1)S(1)} %slice.182), channel_id=1, source_target_pairs={{0,4},{4,8},{8,12},{1,5},{5,9},{9,13},{2,6},{6,10},{10,14},{3,7},{... | collective-permute-start | bytes 9224 | tf_op jit(solution)/shard_map/ppermute | solution.py:18
  13.3 177.4 %collective-permute-start.3 = (bf16[3,1024]{1,0:T(4,128)(2,1)S(1)}, bf16[3,1024]{1,0:T(4,128)(2,1)S(1)}, u32[]{:S(2)}, u32[]{:S(2)}) collective-permute-start(bf16[3,1024]{1,0:T(4,128)(2,1)S(1)} %slice.194), channel_id=1, source_target_pairs={{0,4},{4,8},{8,12},{1,5},{5,9},{9,13},{2,6},{6,10},{10,14},{3,7},{... | collective-permute-start | bytes 18440 | tf_op jit(solution)/shard_map/ppermute | solution.py:18
  29.6 161.1 %copy-start.20 = (bf16[256,1024]{1,0:T(8,128)(2,1)S(1)}, bf16[256,1024]{1,0:T(8,128)(2,1)}, u32[]{:S(2)}) copy-start(bf16[256,1024]{1,0:T(8,128)(2,1)} %param.24) | copy-start | bytes 1572868
  194.3 5.2 %copy-start.4 = (f32[8,4,64,256]{3,2,1,0:T(8,128)}, f32[8,4,64,256]{3,2,1,0:T(8,128)S(1)}, u32[]{:S(2)}) copy-start(f32[8,4,64,256]{3,2,1,0:T(8,128)S(1)} %fusion.39) | copy-start | bytes 6291460
  231.9 95.4 %all-gather.11.cloned.1.call-start = ((), (), s32[]{:S(2)}) async-start(), calls=%async_computation.1 | async-start | bytes 2621440 | tf_op jit(solution)/shard_map/all_gather | solution.py:23
  232.6 205.9 %all-gather.13.cloned.1.call-start = ((), (), s32[]{:S(2)}) async-start(), calls=%async_computation.2 | async-start | bytes 2621440 | tf_op jit(solution)/shard_map/all_gather | solution.py:23
  236.1 4.1 copy-start.8
  333.1 4.4 copy-start.17
  333.1 4.4 copy-start.19
  337.6 4.6 copy-start.11
  337.6 4.6 copy-start.24
  342.1 4.5 copy-start.21
  342.7 3.9 collective-permute-start.4
  347.7 4.4 collective-permute-start.5
  356.7 5.2 %copy-start.6 = (f32[8,4,64,256]{3,2,1,0:T(8,128)}, f32[8,4,64,256]{3,2,1,0:T(8,128)S(1)}, u32[]{:S(2)}) copy-start(f32[8,4,64,256]{3,2,1,0:T(8,128)S(1)} %fusion.38) | copy-start | bytes 6291460
  393.9 90.7 %all-gather.15.cloned.1.call-start = ((), (), s32[]{:S(2)}) async-start(), calls=%async_computation.3 | async-start | bytes 2621440 | tf_op jit(solution)/shard_map/all_gather | solution.py:23
  484.6 6.0 %copy-start.13 = (f32[4,8,128,128]{2,3,1,0:T(8,128)S(1)}, f32[4,8,128,128]{2,3,1,0:T(8,128)}, u32[]{:S(2)}) copy-start(f32[4,8,128,128]{2,3,1,0:T(8,128)} %get-tuple-element.283) | copy-start | bytes 6291460
  490.6 3.8 copy-start.16
  490.6 3.8 copy-start.18
  494.4 4.6 copy-start.12
  (11 other events, 18.6 us)
Sparse Core Ops, SparseCore 0:
  232.0 49.0 all-gather.8
  282.7 44.6 all-gather.10
  394.0 44.4 all-gather.12
  439.9 44.6 all-gather.14
where the time goes:
time: 517 us; the launch traced here: 507 us
  other arithmetic  179 us (35%)
  waiting for transfers between devices  175 us (34%)
  matrix products  97.5 us (19%)
  local copies, waits for them, and re-layouts  33 us (6%)
  between operations  14.2 us (3%)
  starting transfers between devices  8 us (2%)
    all_gather x4, waiting for transfers between devices, carried_in(): pieces = jax.tree.map(lambda part: lax.all_gather(part, axis), value)  168 us
    another operation x3, other arithmetic, mixer_part(): jax.scipy.linalg.solve_triangular(system, right_side, lower=True, unit_di...  158 us
    dot_general x14, matrix products, compose(): jnp.einsum('hab,hbc->hac', later[0], earlier[1], precision=highest_precis...  26.2 us
    dynamic_update_slice x24, local copies, waits for them, and re-layouts, mixer_part(): lax.scan(advance, identity_pair, (operator.transpose(1, 0, 2, 3), state_e...  15.2 us
    dot_general x8, matrix products, compose(): jnp.einsum('hab,hbc->hac', later[0], earlier[0], precision=highest_precis...  13.6 us
    dot_general x2, matrix products, mixer_part(): jnp.einsum('hnjd,hnje->hnde', key_end, weight_rows, precision=highest_pre...  10.6 us
    dot_general x2, matrix products, mixer_part(): jnp.einsum('hnjd,hnje->hnde', key_end, value_rows, precision=highest_prec...  10.3 us
  transfers between devices with their start and end apart: 10, of which 6 were waited for; matrix products, arithmetic and copies ran while one was open for 38% of the time, Pallas kernels for 0%

commit v1 on v0

v1 whole, which is shorter than its diff:
```python
import functools

import jax
import jax.numpy as jnp
from jax import lax
from jax.experimental import pallas as pl
from jax.experimental.pallas import tpu as pltpu
from jax.sharding import PartitionSpec as P

D = 128
RIM = 16
CONV = 4
SIZES = (1, 2, 4, 8, 16, 32, 64)
bf16 = jnp.bfloat16
f32 = jnp.float32
MESH = pl.DeviceIdType.MESH


def split(x):
    high = x.astype(bf16)
    return high, (x - high.astype(f32)).astype(bf16)


def dot(a, b):
    return jnp.dot(a, b, preferred_element_type=f32)


def dot_nt(a, b):
    return lax.dot_general(a, b, (((1,), (1,)), ((), ())), preferred_element_type=f32)


def mm(a, b, one=dot):
    return one(a[0], b[0]) + (one(a[0], b[1]) + one(a[1], b[0]))


def sigmoid(x):
    return 1.0 / (1.0 + jnp.exp(-x))


def iota(shape, dim):
    return lax.broadcasted_iota(jnp.int32, shape, dim)


def inverses(parts, mask):
    eye = (iota((D, D), 0) == iota((D, D), 1)).astype(f32)
    inv = [eye - a * mask[0] for a in parts]
    for i in range(1, len(SIZES)):
        halves = [split(t) for t in inv]
        lower = [split(a * mask[i]) for a in parts]
        mid = [split(mm(t, a)) for t, a in zip(halves, lower)]
        inv = [t - mm(m, h) for t, m, h in zip(inv, mid, halves)]
    return inv


def kernel(
    nctx, q_in, k_in, v_in, g_in, dw_in, small_in, seg_in, out,
    qbuf, kbuf, vbuf, gbuf, dw, small, seg, segp, o1,
    xs, segx, keep, pair, dmask, cum, cumt, beta, betat,
    zh, zl, yh, yl, bv, s_in, s_out,
    loc_sem, x_send, x_recv, r_send, r_recv, c_send, c_recv, o_send, o_recv, o_loc, v_send, v_recv,
):
    T = q_in.shape[1]
    HQ = q_in.shape[2] // 2
    HV = v_in.shape[1] // 2
    NH = HV // D
    NK = HQ // D
    REP = NH // NK
    s = lax.axis_index("section")
    o = 1 - s
    c = lax.axis_index("ctx")
    has_prev = c > 0
    has_next = c < nctx - 1

    def cols(half, width):
        return pl.ds(pl.multiple_of(half * width, width), width)

    body = pl.ds(RIM, T)
    tail = pl.ds(T - RIM, RIM)
    rim = pl.ds(0, RIM)

    local = [
        (q_in.at[0, :, cols(s, HQ)], qbuf.at[s, body]),
        (k_in.at[0, :, cols(s, HQ)], kbuf.at[s, body]),
        (g_in.at[0, :, cols(s, HV)], gbuf.at[s]),
        (v_in.at[:, cols(s, HV)], vbuf.at[0, body]),
        (dw_in, dw.at[s]),
        (small_in, small.at[s]),
        (seg_in, seg),
    ]
    local = [pltpu.make_async_copy(a, b, loc_sem.at[i]) for i, (a, b) in enumerate(local)]
    for cp in local:
        cp.start()

    barrier = pltpu.get_barrier_semaphore()
    pl.semaphore_signal(barrier, inc=1, device_id={"section": o}, device_id_type=MESH)
    for ok, other in ((has_prev, c - 1), (has_next, c + 1)):

        @pl.when(ok)
        def _():
            for sec in (s, o):
                pl.semaphore_signal(
                    barrier, inc=1, device_id={"ctx": other, "section": sec}, device_id_type=MESH
                )

    pl.semaphore_wait(
        barrier, 1 + 2 * has_prev.astype(jnp.int32) + 2 * has_next.astype(jnp.int32)
    )

    def remote(src, dst, send, recv, where):
        return pltpu.make_async_remote_copy(
            src_ref=src, dst_ref=dst, send_sem=send, recv_sem=recv,
            device_id=where, device_id_type=MESH,
        )

    partner = {"section": o}
    ahead = {"ctx": c + 1}
    ahead_o = {"ctx": c + 1, "section": o}
    swaps = [
        (dw_in, dw.at[s]),
        (small_in, small.at[s]),
        (k_in.at[0, :, cols(o, HQ)], kbuf.at[s, body]),
        (q_in.at[0, :, cols(o, HQ)], qbuf.at[s, body]),
        (g_in.at[0, :, cols(o, HV)], gbuf.at[s]),
    ]
    swaps = [
        remote(a, b, x_send.at[i], x_recv.at[i], partner) for i, (a, b) in enumerate(swaps)
    ]
    rims = [
        (seg_in, segp, ahead),
        (k_in.at[0, tail, cols(s, HQ)], kbuf.at[s, rim], ahead),
        (q_in.at[0, tail, cols(s, HQ)], qbuf.at[s, rim], ahead),
        (k_in.at[0, tail, cols(o, HQ)], kbuf.at[s, rim], ahead_o),
        (q_in.at[0, tail, cols(o, HQ)], qbuf.at[s, rim], ahead_o),
        (v_in.at[tail, cols(s, HV)], vbuf.at[0, rim], ahead),
    ]
    rims = [
        remote(a, b, r_send.at[i], r_recv.at[i], w) for i, (a, b, w) in enumerate(rims)
    ]

    @pl.when(has_next)
    def _():
        for cp in rims:
            cp.start()

    for cp in swaps:
        cp.start()

    @pl.when(jnp.logical_not(has_prev))
    def _():
        segp[...] = jnp.zeros_like(segp)
        for layer in range(2):
            kbuf[layer, 0:RIM, :] = jnp.zeros((RIM, HQ), bf16)
            qbuf[layer, 0:RIM, :] = jnp.zeros((RIM, HQ), bf16)
            vbuf[layer, 0:RIM, :] = jnp.zeros((RIM, HV), bf16)
            for h in range(NH):
                s_in[layer, h] = jnp.zeros((D, D), f32)

    row = iota((D, D), 0)
    col = iota((D, D), 1)
    for i, size in enumerate(SIZES):
        down = row // size
        right = col // size
        dmask[i] = jnp.where((down == right + 1) & (down % 2 == 1), 1.0, 0.0)
    trow = iota((T, T), 0)
    tcol = iota((T, T), 1)

    for cp in local:
        cp.wait()
    for cp in swaps:
        cp.wait_recv()

    @pl.when(has_prev)
    def _():
        for cp in rims:
            cp.wait_recv()

    seg_row = seg[0:1, :].astype(f32)
    before = jnp.transpose(jnp.broadcast_to(segp[0:1, :].astype(f32), (D, T)))
    own = jnp.transpose(jnp.broadcast_to(seg_row, (D, T)))
    segx[0:RIM, :] = before[T - RIM :, :]
    segx[RIM:, :] = own
    for j in range(CONV - 1):
        keep[j] = jnp.where(segx[RIM - 3 + j : RIM - 3 + j + T, :] == own, 1.0, 0.0)
    last = before[T - 1 : T, :]
    keep[CONV - 1] = jnp.where(own == last, 1.0, 0.0)
    own_wide = jnp.concatenate([own] * (T // D), axis=1)
    pair[...] = jnp.where((own_wide == seg_row) & (trow >= tcol), 1.0, 0.0)

    lane = iota((T, D), 1)
    tri = jnp.where(trow >= tcol, 1.0, 0.0).astype(bf16)
    for layer in range(2):
        x = dw[layer]
        rate = small[layer, 5:6, 0:D]
        soft = jnp.maximum(x, 0.0) + jnp.log1p(jnp.exp(-jnp.abs(x)))
        decay = jnp.where(lane < 2 * NH, jnp.maximum(-jnp.exp(rate) * soft, -104.0), 0.0)
        p0 = decay.astype(bf16)
        rest = decay - p0.astype(f32)
        p1 = rest.astype(bf16)
        p2 = (rest - p1.astype(f32)).astype(bf16)
        total = dot(tri, p0) + (dot(tri, p1) + dot(tri, p2))
        cum[layer] = total
        cumt[layer] = jnp.transpose(total)
        b = sigmoid(x)
        beta[layer] = b
        betat[layer] = jnp.transpose(b)

    def conv(x, slot, taps):
        xs[slot] = x.astype(f32)
        total = xs[slot, RIM : RIM + T, :] * taps[CONV - 1 : CONV]
        for j in range(CONV - 1):
            total = total + xs[slot, RIM - 3 + j : RIM - 3 + j + T, :] * keep[j] * taps[j : j + 1]
        return total * sigmoid(total)

    def unit(x):
        return x * lax.rsqrt(jnp.sum(x * x, axis=-1, keepdims=True) + 1e-6)

    def prep(step, carry):
        layer = step // NK
        j = step % NK
        here = pl.ds(pl.multiple_of(j * D, D), D)
        key_at = pl.ds(pl.multiple_of(s * HQ + j * D, D), D)
        kcol = pl.ds(pl.multiple_of(2 * HQ + s * HQ + j * D, D), D)
        kn = unit(conv(kbuf[layer, :, here], 0, small[layer, 0:8, kcol]))
        qn = unit(conv(qbuf[layer, :, here], 1, small[layer, 0:8, key_at]))
        ks, qs = split(kn), split(qn)
        gram = mm(ks, ks, dot_nt)
        qk = mm(qs, ks, dot_nt)
        knt = jnp.transpose(kn)
        parts, held = [], []
        for u in range(REP):
            h = j * REP + u
            hh = s * NH + h
            cc = jnp.sum(jnp.where(lane == hh, cum[layer], 0.0), axis=1, keepdims=True)
            bc = jnp.sum(jnp.where(lane == hh + 2 * NH, beta[layer], 0.0), axis=1, keepdims=True)
            cr = cumt[layer, pl.ds(hh, 1), :]
            br = betat[layer, pl.ds(hh + 2 * NH, 1), :]
            decay = jnp.where(pair[...] > 0.0, jnp.exp(cc - cr), 0.0)
            low = jnp.where(trow > tcol, bc * gram * decay, 0.0)
            fs = jnp.exp(cc) * keep[CONV - 1]
            held.append((h, br, decay, fs, low))
            for i in range(T // D):
                parts.append(low[i * D : (i + 1) * D, i * D : (i + 1) * D])
        inv = inverses(parts, [dmask[i] for i in range(len(SIZES))])
        for u in range(REP):
            h, br, decay, fs, low = held[u]
            t1, t2 = inv[2 * u], inv[2 * u + 1]
            t21 = -mm(split(mm(split(t2), split(low[D:, :D]))), split(t1))
            top = jnp.concatenate([t1, jnp.zeros((D, D), f32)], axis=1)
            bottom = jnp.concatenate([t21, t2], axis=1)
            r = split(jnp.concatenate([top, bottom], axis=0) * br)
            z = split(
                mm(split(jnp.concatenate([decay * qk, knt * decay[T - 1 : T, :]], axis=0)), r)
            )
            eye = jnp.where(row == col, fs[T - 1 : T, :], 0.0)
            y = jnp.concatenate([fs * qn, eye], axis=0) - mm(z, split(fs * kn))
            zh[layer, h], zl[layer, h] = z
            yh[layer, h], yl[layer, h] = split(y)
        return carry

    lax.fori_loop(0, 2 * NK, prep, 0)

    out_copies = []
    for layer in range(2):
        src = vbuf.at[1, body] if layer == 0 else o1
        chain = [
            remote(
                s_out.at[layer, h], s_in.at[layer, h],
                c_send.at[layer, h], c_recv.at[layer, h], ahead,
            )
            for h in range(NH)
        ]
        if layer == 1:

            @pl.when(has_prev)
            def _():
                rim1.wait_recv()

        for h in range(NH):
            tcols = pl.ds(pl.multiple_of(4 * HQ + s * HV + h * D, D), D)
            v = split(conv(vbuf[layer, :, h * D : (h + 1) * D], h, small[layer, 0:8, tcols]))
            bv[h] = mm((zh[layer, h], zl[layer, h]), v)
        for h in range(NH):

            @pl.when(has_prev)
            def _():
                chain[h].wait_recv()

            start = split(s_in[layer, h])
            s_out[layer, h] = bv[h, T:, :] + mm((yh[layer, h, T:, :], yl[layer, h, T:, :]), start)

            @pl.when(has_next)
            def _():
                chain[h].start()

        gain = small[layer, 4:5, 0:D]
        for h in range(NH):
            start = split(s_in[layer, h])
            mixed = bv[h, :T, :] + mm((yh[layer, h, :T, :], yl[layer, h, :T, :]), start)
            scale = lax.rsqrt(jnp.mean(mixed * mixed, axis=-1, keepdims=True) + 1e-6)
            g = gbuf[layer, :, h * D : (h + 1) * D].astype(f32)
            value = (mixed * scale * gain * (g * sigmoid(g))).astype(bf16)
            if layer == 0:
                vbuf[1, RIM:, h * D : (h + 1) * D] = value
            else:
                o1[:, h * D : (h + 1) * D] = value
        if layer == 0:
            rim1 = remote(vbuf.at[1, pl.ds(T, RIM)], vbuf.at[1, rim], v_send, v_recv, ahead)

            @pl.when(has_next)
            def _():
                rim1.start()

        across = remote(src, out.at[0, :, cols(s, HV)], o_send, o_recv, partner)
        along = pltpu.make_async_copy(src, out.at[0, :, cols(s, HV)], o_loc)
        out_copies.append((chain, across, along))

        @pl.when(s == layer)
        def _():
            along.start()

        @pl.when(s != layer)
        def _():
            across.start()

    across, along = out_copies[1][1:]
    across.wait_recv()
    across.wait_send()
    along.wait()

    @pl.when(has_next)
    def _():
        for cp in rims:
            cp.wait_send()
        rim1.wait_send()
        for chain, _, _ in out_copies:
            for cp in chain:
                cp.wait_send()

    for cp in swaps:
        cp.wait_send()


def local(
    nctx, queries_in, keys_in, values_in, gate_in, decay_in, write_in, decay_log,
    conv_query, conv_key, conv_value, norm_gain, segment_ids,
):
    T = segment_ids.shape[0]
    heads = decay_in.shape[2]
    hq = queries_in.shape[2] // 2
    hv = values_in.shape[1] // 2
    nh = heads // 2
    dw = jnp.concatenate(
        [decay_in[0], write_in[0], jnp.zeros((T, D - 2 * heads), f32)], axis=1
    )
    taps = jnp.concatenate([conv_query[0], conv_key[0], conv_value[0]], axis=1).astype(f32)
    width = taps.shape[1]
    small = jnp.concatenate(
        [
            taps,
            jnp.pad(norm_gain, ((0, 0), (0, width - norm_gain.shape[1]))),
            jnp.pad(decay_log, ((0, 0), (0, width - heads))),
            jnp.zeros((2, width), f32),
        ],
        axis=0,
    )
    seg = jnp.broadcast_to(segment_ids[None], (8, T))
    dma = pltpu.SemaphoreType.DMA
    V = pltpu.VMEM
    return pl.pallas_call(
        functools.partial(kernel, nctx),
        out_shape=jax.ShapeDtypeStruct((1, T, 2 * hv), bf16),
        in_specs=[pl.BlockSpec(memory_space=pl.ANY)] * 7,
        out_specs=pl.BlockSpec(memory_space=pl.ANY),
        scratch_shapes=[
            V((2, RIM + T, hq), bf16),
            V((2, RIM + T, hq), bf16),
            V((2, RIM + T, hv), bf16),
            V((2, T, hv), bf16),
            V((2, T, D), f32),
            V((2, 8, width), f32),
            V((8, T), jnp.int32),
            V((8, T), jnp.int32),
            V((T, hv), bf16),
            V((nh, RIM + T, D), f32),
            V((RIM + T, D), f32),
            V((CONV, T, D), f32),
            V((T, T), f32),
            V((len(SIZES), D, D), f32),
            V((2, T, D), f32),
            V((2, D, T), f32),
            V((2, T, D), f32),
            V((2, D, T), f32),
            V((2, nh, T + D, T), bf16),
            V((2, nh, T + D, T), bf16),
            V((2, nh, T + D, D), bf16),
            V((2, nh, T + D, D), bf16),
            V((nh, T + D, D), f32),
            V((2, nh, D, D), f32),
            V((2, nh, D, D), f32),
            dma((7,)),
            dma((5,)),
            dma((5,)),
            dma((6,)),
            dma((6,)),
            dma((2, nh)),
            dma((2, nh)),
            dma,
            dma,
            dma,
            dma,
            dma,
        ],
        compiler_params=pltpu.CompilerParams(
            collective_id=0, has_side_effects=True, vmem_limit_bytes=48 * 2**20
        ),
        name="mixer",
    )(queries_in, keys_in, values_in, gate_in, dw, small, seg)


def solution(mesh):
    placed = (
        P("section", ("groups", "ctx"), "head"),
        P("section", ("groups", "ctx"), "head"),
        P(("groups", "ctx"), "head"),
        P("section", ("groups", "ctx"), "head"),
        P("section", ("groups", "ctx"), "head"),
        P("section", ("groups", "ctx"), "head"),
        P("section", "head"),
        P("section", None, "head"),
        P("section", None, "head"),
        P("section", None, "head"),
        P("section", None),
        P(("groups", "ctx")),
    )
    return jax.shard_map(
        functools.partial(local, mesh.shape["ctx"]),
        mesh=mesh,
        in_specs=placed,
        out_specs=P("section", ("groups", "ctx"), "head"),
        check_vma=False,
    )
```

time: 517 us -> 53.5 us (0.10); the launches traced: 507 us -> 53.1 us
  other arithmetic: 179 us -> 1.58 us
  waiting for transfers between devices: 175 us -> 0 us
  matrix products: 97.5 us -> 0 us
  Pallas kernels: 0 us -> 46.1 us
  local copies, waits for them, and re-layouts: 33 us -> 5.31 us
  between operations: 14.2 us -> 0.07 us
  starting transfers between devices: 8 us -> 0 us
    all_gather x4 -> x0, waiting for transfers between devices: 168 us -> none  [carried_in(): pieces = jax.tree.map(lambda part: lax.all_gather(part, axis), value)]
    another operation x4 -> x0, other arithmetic: 159 us -> none  [the longest x3 158 us: mixer_part(): jax.scipy.linalg.solve_triangular(system, right_side, lower=True, unit_di...]
    dot_general x36 -> x0, matrix products: 93.5 us -> none  [the longest x14 26.2 us: compose(): jnp.einsum('hab,hbc->hac', later[0], earlier[1], precision=highest_precis...]
    pallas_call x0 -> x1, Pallas kernels: none -> 46.1 us  [local(): pl.pallas_call(functools.partial(kernel, nctx), out_shape=jax.ShapeDtypeS...]
    dynamic_update_slice x24 -> x0, local copies, waits for them, and re-layouts: 15.2 us -> none  [mixer_part(): lax.scan(advance, identity_pair, (operator.transpose(1, 0, 2, 3), state_e...]
    ppermute x6 -> x0, starting transfers between devices: 7.88 us -> none  [from_behind(): return lax.ppermute(block, axis, route)]
    another operation x5 -> x0, local copies, waits for them, and re-layouts: 6.5 us -> none
    ppermute x6 -> x0, waiting for transfers between devices: 5.56 us -> none  [from_behind(): return lax.ppermute(block, axis, route)]
  transfers between devices with their start and end apart: 10 -> 0, of which waited for: 6 -> 0; matrix products, arithmetic and copies ran while one was open for 38% -> 0% of each run, Pallas kernels for 0% -> 0%
where the time goes in v1:
time: 53.5 us; the launch traced here: 53.1 us
  Pallas kernels  46.1 us (86%)
  local copies, waits for them, and re-layouts  5.31 us (10%)
  other arithmetic  1.58 us (3%)
    pallas_call x1, Pallas kernels, local(): pl.pallas_call(functools.partial(kernel, nctx), out_shape=jax.ShapeDtypeS...  46.1 us
    unnamed x11, local copies, waits for them, and re-layouts  4.47 us

profile of v1, /device:TPU:29, one launch (start us, length us, event | category | flops | bytes accessed | tf_op | source)
XLA Modules:
  0.0 53.1 jit_solution(17827057030090379047)
XLA Ops:
  0.0 0.0 copy-start
  0.0 0.1 pad.13.clone
  0.1 0.1 pad.19.clone
  0.2 0.7 %broadcast_in_dim.14.seg_in = s32[8,256]{1,0:T(8,128)S(1)} broadcast(s32[256]{0:T(256)} %param.23), dimensions={1} | broadcast | bytes 9216 | tf_op jit(solution)/shard_map/broadcast_in_dim | solution.py:366
  0.8 0.7 %maximum_convert_fusion = f32[4,2048]{1,0:T(4,128)S(1)} fusion(bf16[4,1024]{1,0:T(4,128)(2,1)} %bitcast.7, bf16[4,512]{1,0:T(4,128)(2,1)} %bitcast.8, bf16[4,512]{1,0:T(4,128)(2,1)} %bitcast.9), kind=kLoop, calls=%fused_computation.10 | loop fusion | flops 49152 | bytes 49152 | tf_op jit(solution)/shard_map/convert_element_type | solution.py:355
  1.6 0.7 %fusion.small_in = f32[8,2048]{1,0:T(8,128)S(1)} fusion(f32[1,8]{1,0:T(1,128)} %param.18, f32[1,128]{1,0:T(1,128)} %param.22, f32[4,2048]{1,0:T(4,128)S(1)} %maximum_convert_fusion, f32[8]{0:T(128)S(1)} %pad.13.clone), kind=kLoop, calls=%fused_computation.6 | loop fusion | flops 180224 | bytes 98880 | tf_op jit(solution)/shard_map/concatenate | solution.py:357
  2.3 0.8 %copy.13 = f32[1,256,8]{2,1,0:T(8,128)S(1)} copy(f32[1,256,8]{1,2,0:T(8,128)} %param.16) | data formatting | bytes 16384 | tf_op args[4]
  3.1 0.0 copy-start.2
  3.2 0.9 %copy.14 = f32[1,256,8]{2,1,0:T(8,128)S(1)} copy(f32[1,256,8]{1,2,0:T(8,128)} %param.17) | data formatting | bytes 16384 | tf_op args[5]
  4.0 0.1 maximum_maximum_fusion.dw_in
  4.1 0.0 copy-done
  4.1 0.0 copy-done.2
  4.2 0.0 copy-start.1
  4.2 1.0 %copy-done.1 = bf16[1,256,1024]{2,1,0:T(8,128)(2,1)S(1)} copy-done((bf16[1,256,1024]{2,1,0:T(8,128)(2,1)S(1)}, bf16[1,256,1024]{2,1,0:T(8,128)(2,1)}, u32[]{:S(2)}) %copy-start.1) | copy-done | bytes 524312
  5.2 0.0 copy-start.3
  5.2 0.9 %copy-done.3 = bf16[1,256,512]{2,1,0:T(8,128)(2,1)S(1)} copy-done((bf16[1,256,512]{2,1,0:T(8,128)(2,1)S(1)}, bf16[1,256,512]{2,1,0:T(8,128)(2,1)}, u32[]{:S(2)}) %copy-start.3) | copy-done | bytes 262168
  6.2 46.1 %mixer.1 = bf16[1,256,1024]{2,1,0:T(8,128)(2,1)S(1)} custom-call(bf16[1,256,512]{2,1,0:T(8,128)(2,1)S(1)} %copy-done.2, bf16[1,256,512]{2,1,0:T(8,128)(2,1)S(1)} %copy-done.3, bf16[256,1024]{1,0:T(8,128)(2,1)S(1)} %copy-done, bf16[1,256,1024]{2,1,0:T(8,128)(2,1)S(1)} %copy-done.1, f32[256,128]{1,0:T(8,128)S(1)} %maximum_maximum_fusion.dw_in, ...), custom_call_target="tpu_custom_call" | custom-call | tf_op jit(solution)/shard_map/mixer/pallas_call | solution.py:369
  52.3 0.8 %copy.16 = bf16[1,256,1024]{2,1,0:T(8,128)(2,1)} copy(bf16[1,256,1024]{2,1,0:T(8,128)(2,1)S(1)} %mixer.1) | data formatting | bytes 1048576
  (2 shorter events, 0.0 us)
Async XLA Ops:
  0.0 4.1 %copy-start = (bf16[256,1024]{1,0:T(8,128)(2,1)S(1)}, bf16[256,1024]{1,0:T(8,128)(2,1)}, u32[]{:S(2)}) copy-start(bf16[256,1024]{1,0:T(8,128)(2,1)} %v_in.1) | copy-start | bytes 1572868
  3.1 1.0 %copy-start.2 = (bf16[1,256,512]{2,1,0:T(8,128)(2,1)S(1)}, bf16[1,256,512]{2,1,0:T(8,128)(2,1)}, u32[]{:S(2)}) copy-start(bf16[1,256,512]{2,1,0:T(8,128)(2,1)} %q_in.1) | copy-start | bytes 786436
  4.2 1.0 %copy-start.1 = (bf16[1,256,1024]{2,1,0:T(8,128)(2,1)S(1)}, bf16[1,256,1024]{2,1,0:T(8,128)(2,1)}, u32[]{:S(2)}) copy-start(bf16[1,256,1024]{2,1,0:T(8,128)(2,1)} %g_in.1) | copy-start | bytes 1572868
  5.2 0.9 %copy-start.3 = (bf16[1,256,512]{2,1,0:T(8,128)(2,1)S(1)}, bf16[1,256,512]{2,1,0:T(8,128)(2,1)}, u32[]{:S(2)}) copy-start(bf16[1,256,512]{2,1,0:T(8,128)(2,1)} %k_in.1) | copy-start | bytes 786436

commit v2 on v1

--- a/solution.py
+++ b/solution.py
@@ -29,8 +29,16 @@
     return lax.dot_general(a, b, (((1,), (1,)), ((), ())), preferred_element_type=f32)
 
 
-def mm(a, b, one=dot):
-    return one(a[0], b[0]) + (one(a[0], b[1]) + one(a[1], b[0]))
+def mm(a, b):
+    if a[0].shape[1] > D:
+        return dot(a[0], b[0]) + (dot(a[0], b[1]) + dot(a[1], b[0]))
+    both = jnp.concatenate(a, axis=1), jnp.concatenate([b[0], b[0]], axis=0)
+    return dot(*both) + dot(a[0], b[1])
+
+
+def mm_nt(a, b):
+    both = jnp.concatenate(a, axis=1), jnp.concatenate([b[0], b[0]], axis=1)
+    return dot_nt(*both) + dot_nt(a[0], b[1])
 
 
 def sigmoid(x):
@@ -43,17 +51,18 @@
 
 def inverses(parts, mask):
     eye = (iota((D, D), 0) == iota((D, D), 1)).astype(f32)
-    inv = [eye - a * mask[0] for a in parts]
+    inv = [eye - a * mask[0].astype(f32) for a in parts]
+    parts = [split(a) for a in parts]
     for i in range(1, len(SIZES)):
         halves = [split(t) for t in inv]
-        lower = [split(a * mask[i]) for a in parts]
+        lower = [(a[0] * mask[i], a[1] * mask[i]) for a in parts]
         mid = [split(mm(t, a)) for t, a in zip(halves, lower)]
         inv = [t - mm(m, h) for t, m, h in zip(inv, mid, halves)]
     return inv
 
 
 def kernel(
-    nctx, q_in, k_in, v_in, g_in, dw_in, small_in, seg_in, out,
+    nctx, q_in, k_in, v_in, g_in, d_in, w_in, log_in, cq_in, ck_in, cv_in, gain_in, seg_in, out,
     qbuf, kbuf, vbuf, gbuf, dw, small, seg, segp, o1,
     xs, segx, keep, pair, dmask, cum, cumt, beta, betat,
     zh, zl, yh, yl, bv, s_in, s_out,
@@ -83,13 +92,20 @@
         (k_in.at[0, :, cols(s, HQ)], kbuf.at[s, body]),
         (g_in.at[0, :, cols(s, HV)], gbuf.at[s]),
         (v_in.at[:, cols(s, HV)], vbuf.at[0, body]),
-        (dw_in, dw.at[s]),
-        (small_in, small.at[s]),
-        (seg_in, seg),
+        (d_in.at[0], dw.at[s, 0]),
+        (w_in.at[0], dw.at[s, 1]),
     ]
     local = [pltpu.make_async_copy(a, b, loc_sem.at[i]) for i, (a, b) in enumerate(local)]
     for cp in local:
         cp.start()
+
+    taps = (cq_in, ck_in, cv_in)
+    small[s, 0:CONV, :] = jnp.concatenate([t[0].astype(f32) for t in taps], axis=1)
+    small[s, CONV : CONV + 1, 0:D] = gain_in[...]
+    small[s, CONV + 1 : CONV + 2, 0:D] = jnp.broadcast_to(
+        jnp.concatenate([log_in[...], jnp.zeros((1, D - 2 * NH), f32)], axis=1), (1, D)
+    )
+    seg[...] = jnp.broadcast_to(seg_in[...], (8, T))
 
     barrier = pltpu.get_barrier_semaphore()
     pl.semaphore_signal(barrier, inc=1, device_id={"section": o}, device_id_type=MESH)
@@ -116,8 +132,9 @@
     ahead = {"ctx": c + 1}
     ahead_o = {"ctx": c + 1, "section": o}
     swaps = [
-        (dw_in, dw.at[s]),
-        (small_in, small.at[s]),
+        (d_in.at[0], dw.at[s, 0]),
+        (w_in.at[0], dw.at[s, 1]),
+        (small.at[s], small.at[s]),
         (k_in.at[0, :, cols(o, HQ)], kbuf.at[s, body]),
         (q_in.at[0, :, cols(o, HQ)], qbuf.at[s, body]),
         (g_in.at[0, :, cols(o, HV)], gbuf.at[s]),
@@ -126,7 +143,7 @@
         remote(a, b, x_send.at[i], x_recv.at[i], partner) for i, (a, b) in enumerate(swaps)
     ]
     rims = [
-        (seg_in, segp, ahead),
+        (seg, segp, ahead),
         (k_in.at[0, tail, cols(s, HQ)], kbuf.at[s, rim], ahead),
         (q_in.at[0, tail, cols(s, HQ)], qbuf.at[s, rim], ahead),
         (k_in.at[0, tail, cols(o, HQ)], kbuf.at[s, rim], ahead_o),
@@ -160,7 +177,7 @@
     for i, size in enumerate(SIZES):
         down = row // size
         right = col // size
-        dmask[i] = jnp.where((down == right + 1) & (down % 2 == 1), 1.0, 0.0)
+        dmask[i] = jnp.where((down == right + 1) & (down % 2 == 1), 1.0, 0.0).astype(bf16)
     trow = iota((T, T), 0)
     tcol = iota((T, T), 1)
 
@@ -187,22 +204,26 @@
     pair[...] = jnp.where((own_wide == seg_row) & (trow >= tcol), 1.0, 0.0)
 
     lane = iota((T, D), 1)
-    tri = jnp.where(trow >= tcol, 1.0, 0.0).astype(bf16)
+    upper = jnp.where(trow <= tcol, 1.0, 0.0).astype(bf16)
+    fill = jnp.zeros((D - 2 * NH, T), f32)
     for layer in range(2):
-        x = dw[layer]
-        rate = small[layer, 5:6, 0:D]
+        x = dw[layer, 0]
+        rate = jnp.broadcast_to(small[layer, CONV + 1 : CONV + 2, 0:D], (D, D))
+        rate = jnp.transpose(rate)[0 : 2 * NH, 0:1]
         soft = jnp.maximum(x, 0.0) + jnp.log1p(jnp.exp(-jnp.abs(x)))
-        decay = jnp.where(lane < 2 * NH, jnp.maximum(-jnp.exp(rate) * soft, -104.0), 0.0)
-        p0 = decay.astype(bf16)
-        rest = decay - p0.astype(f32)
-        p1 = rest.astype(bf16)
-        p2 = (rest - p1.astype(f32)).astype(bf16)
-        total = dot(tri, p0) + (dot(tri, p1) + dot(tri, p2))
-        cum[layer] = total
-        cumt[layer] = jnp.transpose(total)
-        b = sigmoid(x)
-        beta[layer] = b
-        betat[layer] = jnp.transpose(b)
+        decay = jnp.maximum(-jnp.exp(rate) * soft, -104.0)
+        p0 = decay.astype(bf16).astype(f32)
+        rest = decay - p0
+        p1 = rest.astype(bf16).astype(f32)
+        three = jnp.concatenate([p0, p1, rest - p1, jnp.zeros_like(x)], axis=0).astype(bf16)
+        total = dot(three, upper)
+        n = 2 * NH
+        total = total[0:n] + (total[n : 2 * n] + total[2 * n : 3 * n])
+        cumt[layer] = total
+        cum[layer] = jnp.transpose(jnp.concatenate([total, fill], axis=0))
+        b = sigmoid(dw[layer, 1])
+        betat[layer] = b
+        beta[layer] = jnp.transpose(jnp.concatenate([b, fill], axis=0))
 
     def conv(x, slot, taps):
         xs[slot] = x.astype(f32)
@@ -223,17 +244,17 @@
         kn = unit(conv(kbuf[layer, :, here], 0, small[layer, 0:8, kcol]))
         qn = unit(conv(qbuf[layer, :, here], 1, small[layer, 0:8, key_at]))
         ks, qs = split(kn), split(qn)
-        gram = mm(ks, ks, dot_nt)
-        qk = mm(qs, ks, dot_nt)
+        gram = mm_nt(ks, ks)
+        qk = mm_nt(qs, ks)
         knt = jnp.transpose(kn)
         parts, held = [], []
         for u in range(REP):
             h = j * REP + u
             hh = s * NH + h
             cc = jnp.sum(jnp.where(lane == hh, cum[layer], 0.0), axis=1, keepdims=True)
-            bc = jnp.sum(jnp.where(lane == hh + 2 * NH, beta[layer], 0.0), axis=1, keepdims=True)
+            bc = jnp.sum(jnp.where(lane == hh, beta[layer], 0.0), axis=1, keepdims=True)
             cr = cumt[layer, pl.ds(hh, 1), :]
-            br = betat[layer, pl.ds(hh + 2 * NH, 1), :]
+            br = betat[layer, pl.ds(hh, 1), :]
             decay = jnp.where(pair[...] > 0.0, jnp.exp(cc - cr), 0.0)
             low = jnp.where(trow > tcol, bc * gram * decay, 0.0)
             fs = jnp.exp(cc) * keep[CONV - 1]
@@ -257,41 +278,39 @@
             yh[layer, h], yl[layer, h] = split(y)
         return carry
 
-    lax.fori_loop(0, 2 * NK, prep, 0)
-
-    out_copies = []
-    for layer in range(2):
-        src = vbuf.at[1, body] if layer == 0 else o1
-        chain = [
+    chains = [
+        [
             remote(
                 s_out.at[layer, h], s_in.at[layer, h],
                 c_send.at[layer, h], c_recv.at[layer, h], ahead,
             )
             for h in range(NH)
         ]
-        if layer == 1:
-
-            @pl.when(has_prev)
-            def _():
-                rim1.wait_recv()
-
+        for layer in range(2)
+    ]
+    rim1 = remote(vbuf.at[1, pl.ds(T, RIM)], vbuf.at[1, rim], v_send, v_recv, ahead)
+
+    def increments(layer):
         for h in range(NH):
             tcols = pl.ds(pl.multiple_of(4 * HQ + s * HV + h * D, D), D)
             v = split(conv(vbuf[layer, :, h * D : (h + 1) * D], h, small[layer, 0:8, tcols]))
             bv[h] = mm((zh[layer, h], zl[layer, h]), v)
+
+    def pass_on(layer):
         for h in range(NH):
 
             @pl.when(has_prev)
             def _():
-                chain[h].wait_recv()
+                chains[layer][h].wait_recv()
 
             start = split(s_in[layer, h])
             s_out[layer, h] = bv[h, T:, :] + mm((yh[layer, h, T:, :], yl[layer, h, T:, :]), start)
 
             @pl.when(has_next)
             def _():
-                chain[h].start()
-
+                chains[layer][h].start()
+
+    def finish(layer):
         gain = small[layer, 4:5, 0:D]
         for h in range(NH):
             start = split(s_in[layer, h])
@@ -304,15 +323,14 @@
             else:
                 o1[:, h * D : (h + 1) * D] = value
         if layer == 0:
-            rim1 = remote(vbuf.at[1, pl.ds(T, RIM)], vbuf.at[1, rim], v_send, v_recv, ahead)
 
             @pl.when(has_next)
             def _():
                 rim1.start()
 
+        src = vbuf.at[1, body] if layer == 0 else o1
         across = remote(src, out.at[0, :, cols(s, HV)], o_send, o_recv, partner)
         along = pltpu.make_async_copy(src, out.at[0, :, cols(s, HV)], o_loc)
-        out_copies.append((chain, across, along))
 
         @pl.when(s == layer)
         def _():
@@ -322,7 +340,36 @@
         def _():
             across.start()
 
-    across, along = out_copies[1][1:]
+        return across, along
+
+    lax.fori_loop(0, NK, prep, 0)
+    increments(0)
+
+    @pl.when(c <= 1)
+    def _():
+        pass_on(0)
+
+    lax.fori_loop(NK, NK + NK // 2, prep, 0)
+
+    @pl.when(c == 2)
+    def _():
+        pass_on(0)
+
+    lax.fori_loop(NK + NK // 2, 2 * NK, prep, 0)
+
+    @pl.when(c > 2)
+    def _():
+        pass_on(0)
+
+    finish(0)
+
+    @pl.when(has_prev)
+    def _():
+        rim1.wait_recv()
+
+    increments(1)
+    pass_on(1)
+    across, along = finish(1)
     across.wait_recv()
     across.wait_send()
     along.wait()
@@ -332,7 +379,7 @@
         for cp in rims:
             cp.wait_send()
         rim1.wait_send()
-        for chain, _, _ in out_copies:
+        for chain in chains:
             for cp in chain:
                 cp.wait_send()
 
@@ -345,38 +392,24 @@
     conv_query, conv_key, conv_value, norm_gain, segment_ids,
 ):
     T = segment_ids.shape[0]
-    heads = decay_in.shape[2]
     hq = queries_in.shape[2] // 2
     hv = values_in.shape[1] // 2
-    nh = heads // 2
-    dw = jnp.concatenate(
-        [decay_in[0], write_in[0], jnp.zeros((T, D - 2 * heads), f32)], axis=1
-    )
-    taps = jnp.concatenate([conv_query[0], conv_key[0], conv_value[0]], axis=1).astype(f32)
-    width = taps.shape[1]
-    small = jnp.concatenate(
-        [
-            taps,
-            jnp.pad(norm_gain, ((0, 0), (0, width - norm_gain.shape[1]))),
-            jnp.pad(decay_log, ((0, 0), (0, width - heads))),
-            jnp.zeros((2, width), f32),
-        ],
-        axis=0,
-    )
-    seg = jnp.broadcast_to(segment_ids[None], (8, T))
+    nh = hv // D
+    width = 4 * hq + 2 * hv
     dma = pltpu.SemaphoreType.DMA
     V = pltpu.VMEM
     return pl.pallas_call(
         functools.partial(kernel, nctx),
         out_shape=jax.ShapeDtypeStruct((1, T, 2 * hv), bf16),
-        in_specs=[pl.BlockSpec(memory_space=pl.ANY)] * 7,
+        in_specs=[pl.BlockSpec(memory_space=pl.ANY)] * 6
+        + [pl.BlockSpec(memory_space=pltpu.VMEM)] * 6,
         out_specs=pl.BlockSpec(memory_space=pl.ANY),
         scratch_shapes=[
             V((2, RIM + T, hq), bf16),
             V((2, RIM + T, hq), bf16),
             V((2, RIM + T, hv), bf16),
             V((2, T, hv), bf16),
-            V((2, T, D), f32),
+            V((2, 2, 2 * nh, T), f32),
             V((2, 8, width), f32),
             V((8, T), jnp.int32),
             V((8, T), jnp.int32),
@@ -385,11 +418,11 @@
             V((RIM + T, D), f32),
             V((CONV, T, D), f32),
             V((T, T), f32),
-            V((len(SIZES), D, D), f32),
+            V((len(SIZES), D, D), bf16),
             V((2, T, D), f32),
-            V((2, D, T), f32),
+            V((2, 2 * nh, T), f32),
             V((2, T, D), f32),
-            V((2, D, T), f32),
+            V((2, 2 * nh, T), f32),
             V((2, nh, T + D, T), bf16),
             V((2, nh, T + D, T), bf16),
             V((2, nh, T + D, D), bf16),
@@ -397,9 +430,9 @@
             V((nh, T + D, D), f32),
             V((2, nh, D, D), f32),
             V((2, nh, D, D), f32),
-            dma((7,)),
-            dma((5,)),
-            dma((5,)),
+            dma((6,)),
+            dma((6,)),
+            dma((6,)),
             dma((6,)),
             dma((6,)),
             dma((2, nh)),
@@ -411,10 +444,14 @@
             dma,
         ],
         compiler_params=pltpu.CompilerParams(
-            collective_id=0, has_side_effects=True, vmem_limit_bytes=48 * 2**20
+            collective_id=0, has_side_effects=True, vmem_limit_bytes=60 * 2**20
         ),
         name="mixer",
-    )(queries_in, keys_in, values_in, gate_in, dw, small, seg)
+    )(
+        queries_in, keys_in, values_in, gate_in,
+        jnp.swapaxes(decay_in, 1, 2), jnp.swapaxes(write_in, 1, 2),
+        decay_log, conv_query, conv_key, conv_value, norm_gain, segment_ids.reshape(1, T),
+    )
 
 
 def solution(mesh):

time: 53.5 us -> 47.6 us (0.89)
  local copies, waits for them, and re-layouts: 5.31 us -> 1.87 us
  other arithmetic: 1.58 us -> 0 us
  Pallas kernels: 46.1 us -> 45.5 us
    unnamed x11 -> x1, local copies, waits for them, and re-layouts: 4.47 us -> 1.87 us
    concatenate x2 -> x0, other arithmetic: 0.85 us -> none  [the longest x1 0.74 us: local(): jnp.concatenate([taps, jnp.pad(norm_gain, ((0, 0), (0, width - norm_gain....]
    convert_element_type x1 -> x0, other arithmetic: 0.73 us -> none  [local(): jnp.concatenate([conv_query[0], conv_key[0], conv_value[0]], axis=1)]
    broadcast_in_dim x3 -> x0, local copies, waits for them, and re-layouts: 0.68 us -> none  [the longest x1 0.68 us: local(): seg = jnp.broadcast_to(segment_ids[None], (8, T))]
    pallas_call x1, Pallas kernels: 46.1 us -> 45.5 us  [local(): pl.pallas_call(functools.partial(kernel, nctx), out_shape=jax.ShapeDtypeS...]
where the time goes in v2:
time: 47.6 us; the launch traced here: 47.4 us
  Pallas kernels  45.5 us (96%)
  local copies, waits for them, and re-layouts  1.87 us (4%)
    pallas_call x1, Pallas kernels, local(): pl.pallas_call(functools.partial(kernel, nctx), out_shape=jax.ShapeDtypeS...  45.5 us
    unnamed x1, local copies, waits for them, and re-layouts  1.87 us

profile of v2, /device:TPU:29, one launch (start us, length us, event | category | flops | bytes accessed | tf_op | source)
XLA Modules:
  0.0 47.4 jit_solution(8618607771220639476)
XLA Ops:
  0.0 45.5 %mixer.1 = bf16[1,256,1024]{2,1,0:T(8,128)(2,1)} custom-call(bf16[1,256,512]{2,1,0:T(8,128)(2,1)} %q_in.1, bf16[1,256,512]{2,1,0:T(8,128)(2,1)} %k_in.1, bf16[256,1024]{1,0:T(8,128)(2,1)} %v_in.1, bf16[1,256,1024]{2,1,0:T(8,128)(2,1)} %g_in.1, f32[1,8,256]{2,1,0:T(8,128)} %bitcast.3, f32[1,8,256]{2,1,0:T(8,128)} %bitcast.4, f32[1,8]{1,0:T(1,128)} %log_in.1, ...), custom_call_target="tpu_custom_call" | custom-call | tf_op jit(solution)/shard_map/mixer/pallas_call | solution.py:401
  45.5 1.9 %copy.14 = bf16[1,256,1024]{2,1,0:T(8,128)(2,1)} copy(bf16[1,256,1024]{2,1,0:T(8,128)(2,1)} %mixer.1) | data formatting | bytes 1048576

commit v3 on v2

--- a/solution.py
+++ b/solution.py
@@ -235,37 +235,37 @@
     def unit(x):
         return x * lax.rsqrt(jnp.sum(x * x, axis=-1, keepdims=True) + 1e-6)
 
-    def prep(step, carry):
-        layer = step // NK
-        j = step % NK
-        here = pl.ds(pl.multiple_of(j * D, D), D)
-        key_at = pl.ds(pl.multiple_of(s * HQ + j * D, D), D)
-        kcol = pl.ds(pl.multiple_of(2 * HQ + s * HQ + j * D, D), D)
-        kn = unit(conv(kbuf[layer, :, here], 0, small[layer, 0:8, kcol]))
-        qn = unit(conv(qbuf[layer, :, here], 1, small[layer, 0:8, key_at]))
-        ks, qs = split(kn), split(qn)
-        gram = mm_nt(ks, ks)
-        qk = mm_nt(qs, ks)
-        knt = jnp.transpose(kn)
-        parts, held = [], []
-        for u in range(REP):
-            h = j * REP + u
-            hh = s * NH + h
-            cc = jnp.sum(jnp.where(lane == hh, cum[layer], 0.0), axis=1, keepdims=True)
-            bc = jnp.sum(jnp.where(lane == hh, beta[layer], 0.0), axis=1, keepdims=True)
-            cr = cumt[layer, pl.ds(hh, 1), :]
-            br = betat[layer, pl.ds(hh, 1), :]
-            decay = jnp.where(pair[...] > 0.0, jnp.exp(cc - cr), 0.0)
-            low = jnp.where(trow > tcol, bc * gram * decay, 0.0)
-            fs = jnp.exp(cc) * keep[CONV - 1]
-            held.append((h, br, decay, fs, low))
-            for i in range(T // D):
-                parts.append(low[i * D : (i + 1) * D, i * D : (i + 1) * D])
+    def prep(layer):
+        parts, held, keyed = [], [], []
+        for j in range(NK):
+            here = pl.ds(j * D, D)
+            key_at = pl.ds(pl.multiple_of(s * HQ + j * D, D), D)
+            kcol = pl.ds(pl.multiple_of(2 * HQ + s * HQ + j * D, D), D)
+            kn = unit(conv(kbuf[layer, :, here], 2 * j, small[layer, 0:8, kcol]))
+            qn = unit(conv(qbuf[layer, :, here], 2 * j + 1, small[layer, 0:8, key_at]))
+            ks, qs = split(kn), split(qn)
+            gram = mm_nt(ks, ks)
+            qk = mm_nt(qs, ks)
+            keyed.append((kn, qn, qk, jnp.transpose(kn)))
+            for u in range(REP):
+                h = j * REP + u
+                hh = s * NH + h
+                cc = jnp.sum(jnp.where(lane == hh, cum[layer], 0.0), axis=1, keepdims=True)
+                bc = jnp.sum(jnp.where(lane == hh, beta[layer], 0.0), axis=1, keepdims=True)
+                cr = cumt[layer, pl.ds(hh, 1), :]
+                br = betat[layer, pl.ds(hh, 1), :]
+                decay = jnp.where(pair[...] > 0.0, jnp.exp(cc - cr), 0.0)
+                low = jnp.where(trow > tcol, bc * gram * decay, 0.0)
+                fs = jnp.exp(cc) * keep[CONV - 1]
+                held.append((br, decay, fs, low[D:, :D]))
+                for i in range(T // D):
+                    parts.append(low[i * D : (i + 1) * D, i * D : (i + 1) * D])
         inv = inverses(parts, [dmask[i] for i in range(len(SIZES))])
-        for u in range(REP):
-            h, br, decay, fs, low = held[u]
-            t1, t2 = inv[2 * u], inv[2 * u + 1]
-            t21 = -mm(split(mm(split(t2), split(low[D:, :D]))), split(t1))
+        for h in range(NH):
+            br, decay, fs, low = held[h]
+            kn, qn, qk, knt = keyed[h // REP]
+            t1, t2 = inv[2 * h], inv[2 * h + 1]
+            t21 = -mm(split(mm(split(t2), split(low))), split(t1))
             top = jnp.concatenate([t1, jnp.zeros((D, D), f32)], axis=1)
             bottom = jnp.concatenate([t21, t2], axis=1)
             r = split(jnp.concatenate([top, bottom], axis=0) * br)
@@ -276,7 +276,6 @@
             y = jnp.concatenate([fs * qn, eye], axis=0) - mm(z, split(fs * kn))
             zh[layer, h], zl[layer, h] = z
             yh[layer, h], yl[layer, h] = split(y)
-        return carry
 
     chains = [
         [
@@ -342,22 +341,22 @@
 
         return across, along
 
-    lax.fori_loop(0, NK, prep, 0)
-    increments(0)
-
-    @pl.when(c <= 1)
-    def _():
-        pass_on(0)
-
-    lax.fori_loop(NK, NK + NK // 2, prep, 0)
-
-    @pl.when(c == 2)
-    def _():
-        pass_on(0)
-
-    lax.fori_loop(NK + NK // 2, 2 * NK, prep, 0)
-
-    @pl.when(c > 2)
+    def turn(layer, carry):
+        prep(layer)
+
+        @pl.when(layer == 0)
+        def _():
+            increments(0)
+
+            @pl.when(c <= 1)
+            def _():
+                pass_on(0)
+
+        return carry
+
+    lax.fori_loop(0, 2, turn, 0)
+
+    @pl.when(c > 1)
     def _():
         pass_on(0)
 
@@ -414,7 +413,7 @@
             V((8, T), jnp.int32),
             V((8, T), jnp.int32),
             V((T, hv), bf16),
-            V((nh, RIM + T, D), f32),
+            V((max(nh, 2 * (hq // D)), RIM + T, D), f32),
             V((RIM + T, D), f32),
             V((CONV, T, D), f32),
             V((T, T), f32),

time: 47.6 us -> 44 us (0.924)
  Pallas kernels: 45.5 us -> 41.9 us
    pallas_call x1, Pallas kernels: 45.5 us -> 41.9 us  [local(): pl.pallas_call(functools.partial(kernel, nctx), out_shape=jax.ShapeDtypeS...]
where the time goes in v3:
time: 44 us; the launch traced here: 43.8 us
  Pallas kernels  41.9 us (95%)
  local copies, waits for them, and re-layouts  1.87 us (4%)
    pallas_call x1, Pallas kernels, local(): pl.pallas_call(functools.partial(kernel, nctx), out_shape=jax.ShapeDtypeS...  41.9 us
    unnamed x1, local copies, waits for them, and re-layouts  1.87 us

profile of v3, /device:TPU:29, one launch (start us, length us, event | category | flops | bytes accessed | tf_op | source)
XLA Modules:
  0.0 43.8 jit_solution(16264708840414742691)
XLA Ops:
  0.0 41.9 %mixer.1 = bf16[1,256,1024]{2,1,0:T(8,128)(2,1)} custom-call(bf16[1,256,512]{2,1,0:T(8,128)(2,1)} %q_in.1, bf16[1,256,512]{2,1,0:T(8,128)(2,1)} %k_in.1, bf16[256,1024]{1,0:T(8,128)(2,1)} %v_in.1, bf16[1,256,1024]{2,1,0:T(8,128)(2,1)} %g_in.1, f32[1,8,256]{2,1,0:T(8,128)} %bitcast.3, f32[1,8,256]{2,1,0:T(8,128)} %bitcast.4, f32[1,8]{1,0:T(1,128)} %log_in.1, ...), custom_call_target="tpu_custom_call" | custom-call | tf_op jit(solution)/shard_map/mixer/pallas_call | solution.py:400
  42.0 1.9 %copy.14 = bf16[1,256,1024]{2,1,0:T(8,128)(2,1)} copy(bf16[1,256,1024]{2,1,0:T(8,128)(2,1)} %mixer.1) | data formatting | bytes 1048576
